TPU v7x, 32 devices: a whole 2x2x4 slice. The times are simulated.
32 devices in a mesh: img: 4 (over x, core), blk: 8 (over z, y).
Axes of the slice: x: 2, y: 2, z: 4, core: 2. Of those that a mesh axis runs over, the one named last changes fastest.
Arguments:
- pixels: bfloat16 [16, 10240, 261], P('img', 'blk'), may hold values from -6 to 6
- counts: int32 [16], P('img'), may hold values from 3160 to 10240, as said below
- latents: bfloat16 [16, 512, 1024], P('img', 'blk'), may hold values from -6 to 6
- cotangent: float32 [16, 512, 1024], P('img', 'blk'), may hold values from -6 to 6
- w_query: bfloat16 [1024, 1024], replicated, may hold values from -0.375 to 0.375
- w_key: bfloat16 [261, 1024], replicated, may hold values from -0.375 to 0.375
- w_value: bfloat16 [261, 1024], replicated, may hold values from -0.375 to 0.375
- w_out: bfloat16 [1024, 1024], replicated, may hold values from -4.5 to 4.5
- w_hidden: bfloat16 [1024, 1024], replicated, may hold values from -0.1875 to 0.1875
- w_back: bfloat16 [1024, 1024], replicated, may hold values from -0.1875 to 0.1875
- gain_query: float32 [1024], replicated, may hold values from 0.1 to 1.9
- gain_pixel: float32 [261], replicated, may hold values from 0.1 to 1.9
- gain_mlp: float32 [1024], replicated, may hold values from 0.1 to 1.9
Outputs:
- updated: float32 [16, 512, 1024], P('img', 'blk')
- grad_latents: float32 [16, 512, 1024], P('img', 'blk')
- grad_pixels: float32 [16, 10240, 261], P('img', 'blk')
- grad_w_query: float32 [1024, 1024], replicated
- grad_w_key: float32 [261, 1024], replicated
- grad_w_value: float32 [261, 1024], replicated
- grad_w_out: float32 [1024, 1024], replicated
- grad_w_hidden: float32 [1024, 1024], replicated
- grad_w_back: float32 [1024, 1024], replicated
- grad_gain_query: float32 [1024], replicated
- grad_gain_pixel: float32 [261], replicated
- grad_gain_mlp: float32 [1024], replicated
Inputs may be any that keep to these rules, and one draw needn't show every extreme that they name: `counts`: each image's count is 10240 * s * s // 81 with s one of 5, 7 and 9; of the 4 images that share an index of img (consecutive images), one has s = 9.
All inputs are finite; a program needn't handle non-finite values.
Results may differ from a plain program's by a relative error of at most 0.013.
The roundings to bfloat16 on the way count: a program that leaves them out, or rounds other values in their place, can miss the bound.
Values may be sent and summed in bfloat16 or wider, within the bound.
A program may use at most 192 MiB of HBM per device.

v0:
```python
import math

import jax
import jax.numpy as jnp
from jax import lax
from jax.sharding import PartitionSpec as P

EPSILON = 1e-05
MASKED = -1e30


def joined(x, axis, combine):
    everything = lax.all_gather(x, axis)
    initial = everything[0]

    def lap(k, so_far):
        return combine(so_far, everything[k])

    return lax.fori_loop(1, lax.axis_size(axis), lap, initial)


def in_blocks(x, dim, peers):
    before, after = (x.shape[:dim], x.shape[dim + 1 :])
    return jnp.moveaxis(x.reshape(*before, peers, -1, *after), dim, 0)


def sum_at_owner(x, axis, dim):
    peers = lax.axis_size(axis)
    parts = lax.all_to_all(in_blocks(x, dim, peers), axis, 0, 0, tiled=True)
    return jnp.sum(parts.astype(jnp.float32), axis=0)


def layer_norm(values, gain_vec):
    centered = values - jnp.mean(values, axis=-1, keepdims=True)
    variance = jnp.mean(centered * centered, axis=-1, keepdims=True)
    return centered * lax.rsqrt(variance + EPSILON) * gain_vec


def gelu_exact(values):
    return jax.nn.gelu(values, approximate=False)


def log_add(first_lse, second_lse):
    higher = jnp.maximum(first_lse, second_lse)
    return higher + jnp.log1p(jnp.exp(-jnp.abs(first_lse - second_lse)))


def product(left_mat, right_mat):
    return jnp.dot(left_mat, right_mat, preferred_element_type=jnp.float32)


def product_tn(left_mat, right_mat):
    return lax.dot_general(
        left_mat, right_mat, (((0,), (0,)), ((), ())), preferred_element_type=jnp.float32
    )


def product_nt(left_mat, right_mat):
    return lax.dot_general(
        left_mat, right_mat, (((1,), (1,)), ((), ())), preferred_element_type=jnp.float32
    )


def masked_scores(all_queries, key_rows, valid_rows, scaling):
    raw_scores = product_nt(all_queries, key_rows) * scaling
    return jnp.where(valid_rows[None, :], raw_scores, MASKED)


def body(
    pixels,
    counts,
    latents,
    cotangent,
    w_query,
    w_key,
    w_value,
    w_out,
    w_hidden,
    w_back,
    gain_query,
    gain_pixel,
    gain_mlp,
):
    micro_count, pixel_rows, feature_width = pixels.shape
    model_width = latents.shape[2]
    scaling = 1.0 / math.sqrt(model_width)
    w_pairs = jnp.concatenate([w_key, w_value], axis=1)
    first_pixel = lax.axis_index("blk") * pixel_rows
    positions = first_pixel + jnp.arange(pixel_rows, dtype=jnp.int32)
    grad_query_w = jnp.zeros((model_width, model_width), jnp.float32)
    grad_pair_w = jnp.zeros((feature_width, 2 * model_width), jnp.float32)
    grad_out_w = jnp.zeros((model_width, model_width), jnp.float32)
    grad_hidden_w = jnp.zeros((model_width, model_width), jnp.float32)
    grad_back_w = jnp.zeros((model_width, model_width), jnp.float32)
    grad_gq = jnp.zeros((model_width,), jnp.float32)
    grad_gp = jnp.zeros((feature_width,), jnp.float32)
    grad_gm = jnp.zeros((model_width,), jnp.float32)
    updated_list, latent_grads, pixel_grads = ([], [], [])
    for micro_index in range(micro_count):
        pixel_count = counts[micro_index]
        valid_rows = positions < pixel_count
        latent_in = latents[micro_index].astype(jnp.float32)
        pixel_in = pixels[micro_index].astype(jnp.float32)
        normed_qf, query_pull = jax.vjp(layer_norm, latent_in, gain_query)
        normed_q = normed_qf.astype(jnp.bfloat16)
        queries = product(normed_q, w_query).astype(jnp.bfloat16)
        normed_pf, pixel_pull = jax.vjp(layer_norm, pixel_in, gain_pixel)
        normed_p = normed_pf.astype(jnp.bfloat16)
        pair_rows = product(normed_p, w_pairs).astype(jnp.bfloat16)
        key_rows = pair_rows[:, :model_width]
        value_rows = pair_rows[:, model_width:]
        all_queries = lax.all_gather(queries, "blk", axis=0, tiled=True)
        scores = masked_scores(all_queries, key_rows, valid_rows, scaling)
        highest = jnp.max(scores, axis=1)
        local_lse = highest + jnp.log(jnp.sum(jnp.exp(scores - highest[:, None]), axis=1))
        row_lse = joined(local_lse, "blk", log_add)
        soft_probs = jnp.exp(scores - row_lse[:, None])
        weights_att = soft_probs.astype(jnp.bfloat16)
        attended = sum_at_owner(product(weights_att, value_rows).astype(jnp.bfloat16), "blk", 0)
        attended_b = attended.astype(jnp.bfloat16)
        hidden_in = latent_in + product(attended_b, w_out)
        normed_mf, mlp_pull = jax.vjp(layer_norm, hidden_in, gain_mlp)
        normed_m = normed_mf.astype(jnp.bfloat16)
        pre_act = product(normed_m, w_hidden)
        activated_f, gelu_pull = jax.vjp(gelu_exact, pre_act)
        activated = activated_f.astype(jnp.bfloat16)
        updated_list.append(hidden_in + product(activated, w_back))
        cot_rows = cotangent[micro_index]
        cot_b = cot_rows.astype(jnp.bfloat16)
        grad_back_w = grad_back_w + product_tn(activated, cot_b)
        (grad_pre,) = gelu_pull(product_nt(cot_b, w_back))
        grad_pre_b = grad_pre.astype(jnp.bfloat16)
        grad_hidden_w = grad_hidden_w + product_tn(normed_m, grad_pre_b)
        grad_h_ln, grad_gm_part = mlp_pull(product_nt(grad_pre_b, w_hidden))
        grad_gm = grad_gm + grad_gm_part
        grad_h = cot_rows + grad_h_ln
        grad_h_b = grad_h.astype(jnp.bfloat16)
        grad_out_w = grad_out_w + product_tn(attended_b, grad_h_b)
        grad_att_b = product_nt(grad_h_b, w_out).astype(jnp.bfloat16)
        grad_att_f = grad_att_b.astype(jnp.float32)
        row_dots = jnp.sum(grad_att_f * attended, axis=1)
        all_grad, all_dots = (
            lax.all_gather(grad_att_f.astype(jnp.bfloat16), "blk", axis=0, tiled=True).astype(
                grad_att_f.dtype
            ),
            lax.all_gather(row_dots.astype(jnp.bfloat16), "blk", axis=0, tiled=True).astype(
                row_dots.dtype
            ),
        )
        grad_att_all = all_grad.astype(jnp.bfloat16)
        grad_probs = product_nt(grad_att_all, value_rows)
        grad_values = product_tn(weights_att, grad_att_all)
        grad_scores = (soft_probs * (grad_probs - all_dots[:, None])).astype(jnp.bfloat16)
        grad_keys = product_tn(grad_scores, all_queries) * scaling
        grad_pairs = jnp.concatenate([grad_keys, grad_values], axis=1).astype(jnp.bfloat16)
        grad_queries = sum_at_owner(
            (product(grad_scores, key_rows) * scaling).astype(jnp.bfloat16), "blk", 0
        ).astype(jnp.bfloat16)
        grad_pair_w = grad_pair_w + product_tn(normed_p, grad_pairs)
        grad_pixel_in, grad_gp_part = pixel_pull(product_nt(grad_pairs, w_pairs))
        grad_gp = grad_gp + grad_gp_part
        pixel_grads.append(grad_pixel_in)
        grad_query_w = grad_query_w + product_tn(normed_q, grad_queries)
        grad_lat_q, grad_gq_part = query_pull(product_nt(grad_queries, w_query))
        grad_gq = grad_gq + grad_gq_part
        latent_grads.append(grad_h + grad_lat_q)
    summed = lax.psum(
        (
            grad_query_w,
            grad_pair_w,
            grad_out_w,
            grad_hidden_w,
            grad_back_w,
            grad_gq,
            grad_gp,
            grad_gm,
        ),
        ("img", "blk"),
    )
    pair_sum = summed[1]
    return (
        jnp.stack(updated_list),
        jnp.stack(latent_grads),
        jnp.stack(pixel_grads),
        summed[0],
        pair_sum[:, :model_width],
        pair_sum[:, model_width:],
        summed[2],
        summed[3],
        summed[4],
        summed[5],
        summed[6],
        summed[7],
    )


def solution(mesh):
    in_specs = (
        P("img", "blk", None),
        P("img"),
        P("img", "blk", None),
        P("img", "blk", None),
        P(),
        P(),
        P(),
        P(),
        P(),
        P(),
        P(),
        P(),
        P(),
    )
    out_specs = (
        P("img", "blk", None),
        P("img", "blk", None),
        P("img", "blk", None),
        P(),
        P(),
        P(),
        P(),
        P(),
        P(),
        P(),
        P(),
        P(),
    )
    return jax.shard_map(body, mesh=mesh, in_specs=in_specs, out_specs=out_specs, check_vma=False)
```

profile of v0, /device:TPU:0, one launch (start us, length us, event | category | flops | bytes accessed | tf_op | source)
XLA Modules:
  0.0 996.6 jit_solution(10540268836450648273)
XLA Ops:
  20.2 10.4 %fusion.283 = (bf16[1,1280,261]{1,0,2:T(2,128)(2,1)}, bf16[1,1280,261]{1,0,2:T(2,128)(2,1)S(1)}, bf16[1,1280,261]{1,0,2:T(2,128)(2,1)}, bf16[1,1280,261]{1,0,2:T(2,128)(2,1)S(1)}) fusion(bf16[4,1280,261]{1,0,2:T(4,128)(2,1)} %param.21), kind=kLoop, calls=%fused_computation.484 | loop fusion | bytes 5345280 | tf_op jit(solution)/shard_map/slice | solution.py:103
  34.8 7.0 convolution_convert_fusion
  41.8 4.8 convolution_convert_fusion.1
  49.8 5.0 convolution_convert_fusion.2
  62.4 27.1 %all-gather.7 = f32[8,1,512]{2,1,0:T(1,128)S(1)} all-gather(f32[1,1,512]{2,1,0:T(1,128)S(1)} %bitcast.461), channel_id=5, replica_groups=mesh['img'=4,'blk'=8] {'blk'}, dimensions={0}, use_global_device_ids=true | all-gather | bytes 18432 | tf_op jit(solution)/shard_map/all_gather | solution.py:13
  89.4 8.7 all-gather.21.cloned.1.call-done
  104.0 26.1 %all-gather.6 = f32[8,1,512]{2,1,0:T(1,128)S(1)} all-gather(f32[1,1,512]{2,1,0:T(1,128)S(1)} %bitcast.462), channel_id=4, replica_groups=mesh['img'=4,'blk'=8] {'blk'}, dimensions={0}, use_global_device_ids=true | all-gather | bytes 18432 | tf_op jit(solution)/shard_map/all_gather | solution.py:13
  130.2 9.6 all-gather.19.cloned.1.call-done
  145.6 26.0 %all-gather.5 = f32[8,1,512]{2,1,0:T(1,128)S(1)} all-gather(f32[1,1,512]{2,1,0:T(1,128)S(1)} %bitcast.463), channel_id=3, replica_groups=mesh['img'=4,'blk'=8] {'blk'}, dimensions={0}, use_global_device_ids=true | all-gather | bytes 18432 | tf_op jit(solution)/shard_map/all_gather | solution.py:13
  172.0 5.1 fusion.68
  181.9 5.1 fusion.65
  187.0 15.1 %all-to-all-done.3 = bf16[8,64,1024]{2,1,0:T(8,128)(2,1)} async-done(((bf16[8,64,1024]{2,1,0:T(8,128)(2,1)}), bf16[8,64,1024]{2,1,0:T(8,128)(2,1)}, u32[]{:S(2)}, u32[]{:S(2)}) %all-to-all-start.3) | async-done | bytes 1048608 | tf_op jit(solution)/shard_map/all_to_all | solution.py:29
  206.8 5.2 fusion.62
  214.8 14.6 %all-to-all-done.2 = bf16[8,64,1024]{2,1,0:T(8,128)(2,1)} async-done(((bf16[8,64,1024]{2,1,0:T(8,128)(2,1)}), bf16[8,64,1024]{2,1,0:T(8,128)(2,1)}, u32[]{:S(2)}, u32[]{:S(2)}) %all-to-all-start.2) | async-done | bytes 1048608 | tf_op jit(solution)/shard_map/all_to_all | solution.py:29
  241.7 15.9 %all-to-all-done.1 = bf16[8,64,1024]{2,1,0:T(8,128)(2,1)} async-done(((bf16[8,64,1024]{2,1,0:T(8,128)(2,1)}), bf16[8,64,1024]{2,1,0:T(8,128)(2,1)}, u32[]{:S(2)}, u32[]{:S(2)}) %all-to-all-start.1) | async-done | bytes 1048608 | tf_op jit(solution)/shard_map/all_to_all | solution.py:29
  279.8 5.0 convolution_convert_fusion.3
  293.1 20.3 %all-reduce.6 = (bf16[512]{0:T(512)(128)(2,1)S(1)}, bf16[512]{0:T(512)(128)(2,1)}, bf16[512]{0:T(512)(128)(2,1)}) all-reduce(bf16[512]{0:T(512)(128)(2,1)S(1)} %dynamic-update-slice.1, bf16[512]{0:T(512)(128)(2,1)} %copy-done.130, bf16[512]{0:T(512)(128)(2,1)} %dynamic-update-slice.2), channel_id=1, replica_groups=mesh['img'=4,'blk'=8] {'blk'}, use_global_device_ids=true, to_apply=%add.1 | all-reduce | flops 1536 | bytes 6144
  322.2 4.8 multiply_convert_fusion.4
  343.5 21.3 %all-gather.29.cloned.1.call-done = bf16[512,1024]{1,0:T(8,128)(2,1)} async-done(((bf16[64,1024]{1,0:T(8,128)(2,1)}), bf16[512,1024]{1,0:T(8,128)(2,1)}) %all-gather.29.cloned.1.call-update) | async-done | bytes 1048592 | tf_op jit(solution)/shard_map/all_gather | solution.py:143
  386.2 28.1 %all-gather.27.cloned.1.call-done = bf16[512,1024]{1,0:T(8,128)(2,1)} async-done(((bf16[64,1024]{1,0:T(8,128)(2,1)}), bf16[512,1024]{1,0:T(8,128)(2,1)}) %all-gather.27.cloned.1.call-update) | async-done | bytes 1048592 | tf_op jit(solution)/shard_map/all_gather | solution.py:143
  449.2 5.6 all-to-all-done.5
  478.2 23.2 %all-gather.17.cloned.1.call-done = bf16[512,1024]{1,0:T(8,128)(2,1)} async-done(((bf16[64,1024]{1,0:T(8,128)(2,1)}), bf16[512,1024]{1,0:T(8,128)(2,1)}) %all-gather.17.cloned.1.call-update) | async-done | bytes 1048592 | tf_op jit(solution)/shard_map/all_gather | solution.py:112
  507.2 26.0 %all-gather.4 = f32[8,1,512]{2,1,0:T(1,128)S(1)} all-gather(f32[1,1,512]{2,1,0:T(1,128)S(1)} %bitcast.464), channel_id=2, replica_groups=mesh['img'=4,'blk'=8] {'blk'}, dimensions={0}, use_global_device_ids=true | all-gather | bytes 18432 | tf_op jit(solution)/shard_map/all_gather | solution.py:13
  533.5 5.1 fusion.59
  582.3 19.9 %all-reduce = bf16[512]{0:T(512)(128)(2,1)S(1)} all-reduce(bf16[512]{0:T(512)(128)(2,1)} %dynamic-update-slice), channel_id=1, replica_groups=mesh['img'=4,'blk'=8] {'blk'}, use_global_device_ids=true, to_apply=%add | all-reduce | flops 512 | bytes 2048
  605.2 6.5 add_add_fusion.2
  621.4 4.7 multiply_convert_fusion.7
  630.6 7.8 add_add_fusion.1
  648.5 6.1 all-to-all-done.4
  658.9 5.0 add_add_fusion.3
  689.2 39.7 %all-reduce.4 = (f32[1024]{0:T(1024)}, f32[261]{0:T(512)}, f32[1024]{0:T(1024)}) all-reduce(f32[1024]{0:T(1024)S(1)} %add_add_fusion.17, f32[261]{0:T(512)S(1)} %add_add_fusion.18, f32[1024]{0:T(1024)S(1)} %add_add_fusion.16), channel_id=1, replica_groups=mesh['img'=4,'blk'=8] {'img','blk'}, use_global_device_ids=true, to_apply=%region_85.86 | all-reduce | flops 2309 | bytes 18472 | tf_op jit(solution)/shard_map/psum | solution.py:167
  732.2 241.3 %all-reduce.9.cloned.1.call-done = (f32[1024,1024]{1,0:T(8,128)}, f32[261,2048]{1,0:T(8,128)}, f32[1024,1024]{1,0:T(8,128)}, f32[1024,1024]{1,0:T(8,128)}, f32[1024,1024]{1,0:T(8,128)}) async-done(((f32[1024,1024]{1,0:T(8,128)}, f32[261,2048]{1,0:T(8,128)}, f32[1024,1024]{1,0:T(8,128)}, f32[1024,1024]{1,0:T(8,128)}, f32[1024,1024]{1,0:T(8,128)}), (f32[1024,1024]{1,0:T(8,128)}, f32[261,2048]{1,0:T(8,128)}, ...) | async-done | bytes 18915344 | tf_op jit(solution)/shard_map/psum | solution.py:167
  (650 shorter events, 324.6 us)
Async XLA Ops:
  7.2 232.1 %copy-start = (bf16[1024,1024]{1,0:T(8,128)(2,1)S(1)}, bf16[1024,1024]{1,0:T(8,128)(2,1)}, u32[]{:S(2)}) copy-start(bf16[1024,1024]{1,0:T(8,128)(2,1)} %param.29) | copy-start | bytes 6291460
  7.2 49.3 %all-gather.23.cloned.1.call-start = ((), (), s32[]{:S(2)}) async-start(), calls=%async_computation.11 | async-start | bytes 1179648 | tf_op jit(solution)/shard_map/all_gather | solution.py:112
  13.5 84.7 %all-gather.21.cloned.1.call-start = ((), (), s32[]{:S(2)}) async-start(), calls=%async_computation.10 | async-start | bytes 1179648 | tf_op jit(solution)/shard_map/all_gather | solution.py:112
  16.5 123.3 %all-gather.19.cloned.1.call-start = ((), (), s32[]{:S(2)}) async-start(), calls=%async_computation.9 | async-start | bytes 1179648 | tf_op jit(solution)/shard_map/all_gather | solution.py:112
  16.6 14.1 %copy-start.123 = (f32[64]{0:T(128)}, f32[64]{0:T(128)S(1)}, u32[]{:S(2)}) copy-start(f32[64]{0:T(128)S(1)} %fusion.235) | copy-start | bytes 772
  31.0 10.8 %copy-start.11 = (bf16[1,1280,261]{1,2,0:T(8,128)(2,1)}, bf16[1,1280,261]{1,2,0:T(8,128)(2,1)S(1)}, u32[]{:S(2)}) copy-start(bf16[1,1280,261]{1,2,0:T(8,128)(2,1)S(1)} %get-tuple-element.548) | copy-start | bytes 2004484
  89.4 12.5 %copy-start.95 = (f32[8,1,512]{2,1,0:T(1,128)}, f32[8,1,512]{2,1,0:T(1,128)S(1)}, u32[]{:S(2)}) copy-start(f32[8,1,512]{2,1,0:T(1,128)S(1)} %all-gather.7) | copy-start | bytes 49156
  130.1 13.4 %copy-start.96 = (f32[8,1,512]{2,1,0:T(1,128)}, f32[8,1,512]{2,1,0:T(1,128)S(1)}, u32[]{:S(2)}) copy-start(f32[8,1,512]{2,1,0:T(1,128)S(1)} %all-gather.6) | copy-start | bytes 49156
  143.6 28.0 %slice-start = ((f32[8,1,512]{2,1,0:T(1,128)}), f32[1,1,512]{2,1,0:T(1,128)S(1)}, s32[]{:S(2)}) async-start(f32[8,1,512]{2,1,0:T(1,128)} %copy-done.95), calls=%async_computation.17 | async-start | bytes 4096 | tf_op jit(solution)/shard_map/slice | solution.py:14
  177.1 25.0 %all-to-all-start.3 = ((bf16[8,64,1024]{2,1,0:T(8,128)(2,1)}), bf16[8,64,1024]{2,1,0:T(8,128)(2,1)}, u32[]{:S(2)}, u32[]{:S(2)}) async-start(bf16[8,64,1024]{2,1,0:T(8,128)(2,1)} %bitcast.442), calls=%async_computation.3 | async-start | bytes 2097152 | tf_op jit(solution)/shard_map/all_to_all | solution.py:29
  187.0 19.4 %slice-start.2 = ((f32[8,1,512]{2,1,0:T(1,128)}), f32[1,1,512]{2,1,0:T(1,128)S(1)}, s32[]{:S(2)}) async-start(f32[8,1,512]{2,1,0:T(1,128)} %copy-done.97), calls=%async_computation.19 | async-start | bytes 4096 | tf_op jit(solution)/shard_map/slice | solution.py:14
  202.1 27.2 %all-to-all-start.2 = ((bf16[8,64,1024]{2,1,0:T(8,128)(2,1)}), bf16[8,64,1024]{2,1,0:T(8,128)(2,1)}, u32[]{:S(2)}, u32[]{:S(2)}) async-start(bf16[8,64,1024]{2,1,0:T(8,128)(2,1)} %bitcast.441), calls=%async_computation.2 | async-start | bytes 2097152 | tf_op jit(solution)/shard_map/all_to_all | solution.py:29
  229.4 28.2 %all-to-all-start.1 = ((bf16[8,64,1024]{2,1,0:T(8,128)(2,1)}), bf16[8,64,1024]{2,1,0:T(8,128)(2,1)}, u32[]{:S(2)}, u32[]{:S(2)}) async-start(bf16[8,64,1024]{2,1,0:T(8,128)(2,1)} %bitcast.443), calls=%async_computation.1 | async-start | bytes 2097152 | tf_op jit(solution)/shard_map/all_to_all | solution.py:29
  233.6 84.2 %all-gather.31.cloned.1.call-start = ((), (), s32[]{:S(2)}) async-start(), calls=%async_computation.15 | async-start | bytes 1179648 | tf_op jit(solution)/shard_map/all_gather | solution.py:143
  239.2 31.8 %copy-start.110 = (f32[64]{0:T(128)}, f32[64]{0:T(128)S(1)}, u32[]{:S(2)}) copy-start(f32[64]{0:T(128)S(1)} %fusion.240) | copy-start | bytes 772
  239.3 31.8 %copy-start.117 = (f32[64]{0:T(128)}, f32[64]{0:T(128)S(1)}, u32[]{:S(2)}) copy-start(f32[64]{0:T(128)S(1)} %fusion.238) | copy-start | bytes 772
  274.9 89.9 %all-gather.29.cloned.1.call-start = ((), (), s32[]{:S(2)}) async-start(), calls=%async_computation.14 | async-start | bytes 1179648 | tf_op jit(solution)/shard_map/all_gather | solution.py:143
  327.0 47.6 %all-to-all-start.7 = ((bf16[8,64,1024]{2,1,0:T(8,128)(2,1)}), bf16[8,64,1024]{2,1,0:T(8,128)(2,1)}, u32[]{:S(2)}, u32[]{:S(2)}) async-start(bf16[8,64,1024]{2,1,0:T(8,128)(2,1)} %bitcast.445), calls=%async_computation.7 | async-start | bytes 2097152 | tf_op jit(solution)/shard_map/all_to_all | solution.py:29
  331.3 83.1 %all-gather.27.cloned.1.call-start = ((), (), s32[]{:S(2)}) async-start(), calls=%async_computation.13 | async-start | bytes 1179648 | tf_op jit(solution)/shard_map/all_gather | solution.py:143
  374.6 49.5 %all-to-all-start.6 = ((bf16[8,64,1024]{2,1,0:T(8,128)(2,1)}), bf16[8,64,1024]{2,1,0:T(8,128)(2,1)}, u32[]{:S(2)}, u32[]{:S(2)}) async-start(bf16[8,64,1024]{2,1,0:T(8,128)(2,1)} %bitcast.446), calls=%async_computation.6 | async-start | bytes 2097152 | tf_op jit(solution)/shard_map/all_to_all | solution.py:29
  424.1 30.6 %all-to-all-start.5 = ((bf16[8,64,1024]{2,1,0:T(8,128)(2,1)}), bf16[8,64,1024]{2,1,0:T(8,128)(2,1)}, u32[]{:S(2)}, u32[]{:S(2)}) async-start(bf16[8,64,1024]{2,1,0:T(8,128)(2,1)} %bitcast.444), calls=%async_computation.5 | async-start | bytes 2097152 | tf_op jit(solution)/shard_map/all_to_all | solution.py:29
  428.5 72.9 %all-gather.17.cloned.1.call-start = ((), (), s32[]{:S(2)}) async-start(), calls=%async_computation.8 | async-start | bytes 1179648 | tf_op jit(solution)/shard_map/all_gather | solution.py:112
  475.1 26.3 %copy-start.127 = (pred[1280]{0:T(1024)(128)(4,1)S(1)}, pred[1280]{0:T(1024)(128)(4,1)}, u32[]{:S(2)}) copy-start(pred[1280]{0:T(1024)(128)(4,1)} %fusion.228) | copy-start | bytes 3844
  538.6 24.9 %all-to-all-start = ((bf16[8,64,1024]{2,1,0:T(8,128)(2,1)}), bf16[8,64,1024]{2,1,0:T(8,128)(2,1)}, u32[]{:S(2)}, u32[]{:S(2)}) async-start(bf16[8,64,1024]{2,1,0:T(8,128)(2,1)} %bitcast.448), calls=%async_computation | async-start | bytes 2097152 | tf_op jit(solution)/shard_map/all_to_all | solution.py:29
  542.9 74.1 %all-gather.25.cloned.1.call-start = ((), (), s32[]{:S(2)}) async-start(), calls=%async_computation.12 | async-start | bytes 1179648 | tf_op jit(solution)/shard_map/all_gather | solution.py:143
  626.1 28.5 %all-to-all-start.4 = ((bf16[8,64,1024]{2,1,0:T(8,128)(2,1)}), bf16[8,64,1024]{2,1,0:T(8,128)(2,1)}, u32[]{:S(2)}, u32[]{:S(2)}) async-start(bf16[8,64,1024]{2,1,0:T(8,128)(2,1)} %bitcast.447), calls=%async_computation.4 | async-start | bytes 2097152 | tf_op jit(solution)/shard_map/all_to_all | solution.py:29
  630.5 343.0 %all-reduce.9.cloned.1.call-start = ((), (), s32[]{:S(2)}) async-start(), calls=%async_computation.16 | async-start | bytes 37879808 | tf_op jit(solution)/shard_map/psum | solution.py:167
  670.7 17.3 %copy-start.126 = (f32[64]{0:T(128)}, f32[64]{0:T(128)S(1)}, u32[]{:S(2)}) copy-start(f32[64]{0:T(128)S(1)} %multiply_multiply_fusion.26) | copy-start | bytes 772
  670.7 16.1 %copy-start.142 = (f32[64]{0:T(128)}, f32[64]{0:T(128)S(1)}, u32[]{:S(2)}) copy-start(f32[64]{0:T(128)S(1)} %multiply_multiply_fusion.24) | copy-start | bytes 772
  686.9 41.9 %copy-start.38 = (f32[64,1024]{1,0:T(8,128)S(1)}, f32[64,1024]{1,0:T(8,128)}, u32[]{:S(2)}) copy-start(f32[64,1024]{1,0:T(8,128)} %get-tuple-element.492) | copy-start | bytes 786436
  687.9 41.9 %copy-start.33 = (f32[64,1024]{1,0:T(8,128)S(1)}, f32[64,1024]{1,0:T(8,128)}, u32[]{:S(2)}) copy-start(f32[64,1024]{1,0:T(8,128)} %copy-done.31) | copy-start | bytes 786436
  687.9 41.9 %copy-start.143 = (f32[64]{0:T(128)S(1)}, f32[64]{0:T(128)}, u32[]{:S(2)}) copy-start(f32[64]{0:T(128)} %copy-done.142) | copy-start | bytes 772
  (167 other events, 556.1 us)
Sparse Core Ops, SparseCore 0:
  13.6 42.8 all-gather.22
  59.2 38.9 all-gather.20
  100.9 38.8 all-gather.18
  275.1 39.1 all-gather.30
  316.2 48.5 all-gather.28
  366.8 47.5 all-gather.26
  462.2 39.1 all-gather.16
  576.6 39.1 all-gather.24
  664.1 309.3 all-reduce.8
where the time goes:
time: 1010 us; the launch traced here: 997 us
  waiting for transfers between devices  394 us (39%)
  matrix products  258 us (26%)
  blocking collectives  185 us (18%)
  local copies, waits for them, and re-layouts  64.2 us (6%)
  other arithmetic  41.6 us (4%)
  starting transfers between devices  35.6 us (4%)
  between operations  16.9 us (2%)
    psum x1, waiting for transfers between devices, body(): lax.psum((grad_query_w, grad_pair_w, grad_out_w, grad_hidden_w, grad_back...  241 us
    all_gather x4, blocking collectives, joined(): everything = lax.all_gather(x, axis)  105 us
    dot_general x28, matrix products, product_tn(): lax.dot_general(left_mat, right_mat, (((0,), (0,)), ((), ())), preferred_...  97.9 us
    dot_general x28, matrix products, product(): return jnp.dot(left_mat, right_mat, preferred_element_type=jnp.float32)  87.5 us
    dot_general x28, matrix products, product_nt(): lax.dot_general(left_mat, right_mat, (((1,), (1,)), ((), ())), preferred_...  72.8 us
    all_to_all x8, waiting for transfers between devices, sum_at_owner(): parts = lax.all_to_all(in_blocks(x, dim, peers), axis, 0, 0, tiled=True)  61 us
    all_gather x4, waiting for transfers between devices, body(): lax.all_gather(grad_att_f.astype(jnp.bfloat16), 'blk', axis=0, tiled=True)  49.5 us
    unnamed x377, local copies, waits for them, and re-layouts  47.8 us
  transfers between devices with their start and end apart: 17, of which 13 were waited for; matrix products, arithmetic and copies ran while one was open for 25% of the time, Pallas kernels for 0%

commit v1 on v0

v1 whole, which is shorter than its diff:
```python
import math

import jax
import jax.numpy as jnp
from jax import lax
from jax.sharding import PartitionSpec as P

EPSILON = 1e-05
MASKED = -1e30


def layer_norm(values, gain_vec):
    centered = values - jnp.mean(values, axis=-1, keepdims=True)
    variance = jnp.mean(centered * centered, axis=-1, keepdims=True)
    return centered * lax.rsqrt(variance + EPSILON) * gain_vec


def gelu_exact(values):
    return jax.nn.gelu(values, approximate=False)


def low(values):
    return values.astype(jnp.bfloat16)


def product(left_mat, right_mat):
    return jnp.dot(left_mat, right_mat, preferred_element_type=jnp.float32)


def product_tn(left_mat, right_mat):
    return lax.dot_general(
        left_mat, right_mat, (((0,), (0,)), ((), ())), preferred_element_type=jnp.float32
    )


def product_nt(left_mat, right_mat):
    return lax.dot_general(
        left_mat, right_mat, (((1,), (1,)), ((), ())), preferred_element_type=jnp.float32
    )


def each(spec, left, right):
    return jnp.einsum(spec, left, right, preferred_element_type=jnp.float32)


def to_owner(x, peers):
    micro, rows = x.shape[:2]
    blocks = jnp.moveaxis(x.reshape(micro, peers, rows // peers, *x.shape[2:]), 1, 0)
    return lax.all_to_all(blocks, "blk", 0, 0, tiled=True)


def body(pixels, counts, latents, cotangent, w_query, w_key, w_value, w_out, w_hidden, w_back, gain_query, gain_pixel, gain_mlp):
    micro, pixel_rows, features = pixels.shape
    lat_rows, width = latents.shape[1:]
    peers = lax.axis_size("blk")
    scaling = 1.0 / math.sqrt(width)
    rows = micro * lat_rows
    positions = lax.axis_index("blk") * pixel_rows + jnp.arange(pixel_rows, dtype=jnp.int32)
    valid = positions[None, :] < counts[:, None]

    latent_in = latents.reshape(rows, width).astype(jnp.float32)
    normed_qf, query_pull = jax.vjp(layer_norm, latent_in, gain_query)
    normed_q = low(normed_qf)
    queries = low(product(normed_q, w_query))
    query_feats = low(product_nt(queries, w_key) * scaling).reshape(micro, lat_rows, features)
    all_query = lax.all_gather(query_feats, "blk", axis=1, tiled=True)
    normed_pf, pixel_pull = jax.vjp(layer_norm, pixels.astype(jnp.float32), gain_pixel)
    normed_p = low(normed_pf)
    scores = each("mqf,mpf->mqp", all_query, normed_p)
    scores = jnp.where(valid[:, None, :], scores, MASKED)
    highest = jnp.max(scores, axis=2)
    unscaled = jnp.exp(scores - highest[..., None])
    total = jnp.sum(unscaled, axis=2)
    sums = low(each("mqp,mpf->mqf", low(unscaled), normed_p))
    parts = to_owner(sums, peers).astype(jnp.float32)
    stats = to_owner(jnp.stack([highest, total], axis=2), peers)
    top = jnp.max(stats[..., 0], axis=0)
    scale = jnp.exp(stats[..., 0] - top)
    denom = jnp.sum(stats[..., 1] * scale, axis=0)
    lse = top + jnp.log(denom)
    seen = (jnp.sum(parts * scale[..., None], axis=0) / denom[..., None]).reshape(rows, features)
    seen_b = low(seen)
    attended_b = low(product(seen_b, w_value))
    hidden_in = latent_in + product(attended_b, w_out)
    normed_mf, mlp_pull = jax.vjp(layer_norm, hidden_in, gain_mlp)
    normed_m = low(normed_mf)
    pre_act = product(normed_m, w_hidden)
    activated_f, gelu_pull = jax.vjp(gelu_exact, pre_act)
    activated = low(activated_f)
    updated = hidden_in + product(activated, w_back)
    cot = cotangent.reshape(rows, width)
    cot_b = low(cot)
    grad_back = product_tn(activated, cot_b)
    (grad_pre,) = gelu_pull(product_nt(cot_b, w_back))
    grad_pre_b = low(grad_pre)
    grad_hidden = product_tn(normed_m, grad_pre_b)
    grad_h_ln, grad_gm = mlp_pull(product_nt(grad_pre_b, w_hidden))
    grad_h = cot + grad_h_ln
    grad_h_b = low(grad_h)
    grad_att = low(product_nt(grad_h_b, w_out))
    grad_seen = product_nt(grad_att, w_value)
    dots = jnp.sum(grad_seen * seen, axis=1).reshape(micro, lat_rows)
    value_side = product_tn(seen_b, grad_h_b)
    all_grad = lax.all_gather(low(grad_seen).reshape(micro, lat_rows, features), "blk", axis=1, tiled=True)
    all_stat = lax.all_gather(jnp.stack([lse, dots], axis=2), "blk", axis=1, tiled=True)
    probs = unscaled * jnp.exp(highest - all_stat[..., 0])[..., None]
    grad_probs = each("mqf,mpf->mqp", all_grad, normed_p)
    grad_scores = low(probs * (grad_probs - all_stat[..., 1][..., None]))
    back_sums = low(each("mqp,mpf->mqf", grad_scores, normed_p))
    grad_np = each("mqp,mqf->mpf", low(probs), all_grad) + each("mqp,mqf->mpf", grad_scores, all_query)
    grad_pixels, grad_gp = pixel_pull(grad_np)
    back_feats = jnp.sum(to_owner(back_sums, peers).astype(jnp.float32), axis=0).reshape(rows, features)
    back_b = low(back_feats)
    grad_q = low(product(back_b, w_key) * scaling)
    grad_lat_q, grad_gq = query_pull(product_nt(grad_q, w_query))
    grad_latents = grad_h + grad_lat_q
    query_side = product_tn(normed_q, back_b)
    query_side, value_side, grad_hidden, grad_back, grad_gq, grad_gp, grad_gm = lax.psum(
        (query_side, value_side, grad_hidden, grad_back, grad_gq, grad_gp, grad_gm), ("img", "blk")
    )
    query_b, value_b = low(query_side * scaling), low(value_side)
    return (
        updated.reshape(micro, lat_rows, width),
        grad_latents.reshape(micro, lat_rows, width),
        grad_pixels,
        product(query_b, w_key),
        product_tn(query_b, w_query),
        product_nt(value_b, w_out),
        product_tn(w_value, value_b),
        grad_hidden,
        grad_back,
        grad_gq,
        grad_gp,
        grad_gm,
    )


def solution(mesh):
    spread, same = P("img", "blk", None), P()
    return jax.shard_map(
        body,
        mesh=mesh,
        in_specs=(spread, P("img"), spread, spread) + (same,) * 9,
        out_specs=(spread,) * 3 + (same,) * 9,
        check_vma=False,
    )
```

time: 1010 us -> 493 us (0.49)
  waiting for transfers between devices: 394 us -> 203 us
  matrix products: 258 us -> 87.7 us
  blocking collectives: 185 us -> 91.4 us
  local copies, waits for them, and re-layouts: 64.2 us -> 37.6 us
  starting transfers between devices: 35.6 us -> 14.2 us
    psum x1, waiting for transfers between devices: 241 us -> 104 us  [body(): lax.psum((query_side, value_side, grad_hidden, grad_back, grad_gq, grad_g...]
    dot_general x28 -> x6, matrix products: 97.9 us -> 15.2 us  [product_tn(): lax.dot_general(left_mat, right_mat, (((0,), (0,)), ((), ())), preferred_...]
    dot_general x28 -> x4, matrix products: 87.5 us -> 11.8 us  [product(): return jnp.dot(left_mat, right_mat, preferred_element_type=jnp.float32)]
    all_gather x4 -> x1, blocking collectives: 105 us -> 32.2 us  [body(): lax.all_gather(jnp.stack([lse, dots], axis=2), 'blk', axis=1, tiled=True)]
    dot_general x28 -> x6, matrix products: 72.8 us -> 19.2 us  [product_nt(): lax.dot_general(left_mat, right_mat, (((1,), (1,)), ((), ())), preferred_...]
    all_gather x8 -> x2, waiting for transfers between devices: 92.1 us -> 42.4 us  [the longest x1 42.4 us: body(): all_query = lax.all_gather(query_feats, 'blk', axis=1, tiled=True)]
    dot_general x0 -> x6, matrix products: none -> 41.5 us  [each(): return jnp.einsum(spec, left, right, preferred_element_type=jnp.float32)]
    unnamed x2 -> x0, blocking collectives: 40.1 us -> none
  transfers between devices with their start and end apart: 17 -> 6, of which waited for: 13 -> 4; matrix products, arithmetic and copies ran while one was open for 25% -> 17% of each run, Pallas kernels for 0% -> 0%
where the time goes in v1:
time: 493 us; the launch traced here: 485 us
  waiting for transfers between devices  203 us (41%)
  blocking collectives  91.4 us (19%)
  matrix products  87.7 us (18%)
  local copies, waits for them, and re-layouts  37.6 us (8%)
  other arithmetic  35.8 us (7%)
  between operations  14.8 us (3%)
  starting transfers between devices  14.2 us (3%)
    psum x1, waiting for transfers between devices, body(): lax.psum((query_side, value_side, grad_hidden, grad_back, grad_gq, grad_g...  104 us
    psum x1, blocking collectives, body(): lax.psum((query_side, value_side, grad_hidden, grad_back, grad_gq, grad_g...  59.2 us
    all_to_all x3, waiting for transfers between devices, to_owner(): return lax.all_to_all(blocks, 'blk', 0, 0, tiled=True)  56.3 us
    all_gather x1, waiting for transfers between devices, body(): all_query = lax.all_gather(query_feats, 'blk', axis=1, tiled=True)  42.4 us
    dot_general x6, matrix products, each(): return jnp.einsum(spec, left, right, preferred_element_type=jnp.float32)  41.5 us
    all_gather x1, blocking collectives, body(): lax.all_gather(jnp.stack([lse, dots], axis=2), 'blk', axis=1, tiled=True)  32.2 us
    unnamed x93, local copies, waits for them, and re-layouts  21.9 us
    dot_general x6, matrix products, product_nt(): lax.dot_general(left_mat, right_mat, (((1,), (1,)), ((), ())), preferred_...  19.2 us
  transfers between devices with their start and end apart: 6, of which 4 were waited for; matrix products, arithmetic and copies ran while one was open for 17% of the time, Pallas kernels for 0%

profile of v1, /device:TPU:0, one launch (start us, length us, event | category | flops | bytes accessed | tf_op | source)
XLA Modules:
  0.0 484.5 jit_solution(17341771769472239834)
XLA Ops:
  13.2 2.7 fusion.23
  21.4 42.4 %all-gather.3.cloned.1.call-done = bf16[4,512,261]{2,1,0:T(8,128)(2,1)} async-done(((bf16[4,64,261]{2,1,0:T(8,128)(2,1)}), bf16[4,512,261]{2,1,0:T(8,128)(2,1)}) %all-gather.3.cloned.1.call-update) | async-done | bytes 1069072 | tf_op jit(solution)/shard_map/all_gather | solution.py:66
  63.8 9.3 %select_reduce_fusion = (f32[4,512]{1,0:T(4,128)S(1)}, f32[4,512,1280]{2,1,0:T(8,128)}) fusion(pred[4,1280]{1,0:T(4,128)(4,1)S(1)} %broadcast_compare_fusion, bf16[4,512,261]{2,1,0:T(8,128)(2,1)} %all-gather.3.cloned.1.call-done, f32[261]{0:T(512)S(1)} %copy-done.30, f32[4,1280]{1,0:T(4,128)S(1)} %fusion.50, f32[4,1280]{1,0:T(4,128)S(1)} %broadcast_multiply_fusion, ...), kind=kOutput, calls=%fused_computation.3 | convolution fusion | flops 1380314112 | bytes 14282772 | tf_op jit(solution)/shard_map/mqf,mpf->mqp/dot_general | solution.py:43
  73.1 5.9 %fusion.14 = f32[4,512]{1,0:T(4,128)S(1)} fusion(f32[4,512]{1,0:T(4,128)S(1)} %get-tuple-element.95, f32[4,512,1280]{2,1,0:T(8,128)} %get-tuple-element.96, pred[4,1280]{1,0:T(4,128)(4,1)S(1)} %broadcast_compare_fusion), kind=kLoop, calls=%fused_computation.21 | loop fusion | flops 7862272 | bytes 10507264 | tf_op jit(solution)/shard_map/reduce_sum | solution.py:73
  79.9 3.4 all-to-all-start.1
  83.3 8.4 %fusion.15 = bf16[4,512,261]{1,2,0:T(8,128)(2,1)} fusion(f32[4,512]{1,0:T(4,128)S(1)} %get-tuple-element.95, f32[4,512,1280]{2,1,0:T(8,128)} %get-tuple-element.96, pred[4,1280]{1,0:T(4,128)(4,1)S(1)} %broadcast_compare_fusion, f32[261]{0:T(512)S(1)} %copy-done.30, f32[4,1280]{1,0:T(4,128)S(1)} %fusion.50, f32[4,1280]{1,0:T(4,128)S(1)} %broadcast_multiply_fusion, ...), kind=kOutput, calls=%fused_computation.29 | convolution fusion | flops 1383472128 | bytes 14282772 | tf_op jit(solution)/shard_map/mqp,mpf->mqf/dot_general | solution.py:43
  94.3 2.7 copy.74
  97.1 6.0 %all-to-all-start = ((bf16[8,4,64,261]{3,2,1,0:T(8,128)(2,1)}), bf16[8,4,64,261]{3,2,1,0:T(8,128)(2,1)}, u32[]{:S(2)}, u32[]{:S(2)}) async-start(bf16[8,4,64,261]{3,2,1,0:T(8,128)(2,1)} %copy.74), calls=%async_computation | async-start | bytes 3145728 | tf_op jit(solution)/shard_map/all_to_all | solution.py:49
  105.6 34.0 %all-to-all-done = bf16[8,4,64,261]{3,2,1,0:T(8,128)(2,1)} async-done(((bf16[8,4,64,261]{3,2,1,0:T(8,128)(2,1)}), bf16[8,4,64,261]{3,2,1,0:T(8,128)(2,1)}, u32[]{:S(2)}, u32[]{:S(2)}) %all-to-all-start) | async-done | bytes 1069088 | tf_op jit(solution)/shard_map/all_to_all | solution.py:49
  141.7 2.9 fusion.74
  147.3 3.9 add_convert_fusion
  154.4 3.7 multiply_reduce_fusion.7
  160.1 32.2 %all_gather.10 = f32[4,512,2]{0,2,1:T(2,128)S(1)} all-gather(f32[4,64,2]{0,2,1:T(2,128)S(1)} %copy.78), channel_id=1, replica_groups=mesh['img'=4,'blk'=8] {'blk'}, dimensions={1}, use_global_device_ids=true | all-gather | bytes 18432 | tf_op jit(solution)/shard_map/all_gather | solution.py:105
  199.1 2.8 fusion.79
  201.9 2.9 fusion.64
  204.8 8.6 %multiply_convert_fusion = bf16[4,512,1280]{2,1,0:T(8,128)(2,1)S(1)} fusion(bf16[4,512,261]{2,1,0:T(8,128)(2,1)} %all-gather.5.cloned.1.call-done, f32[4,512]{1,0:T(4,128)S(1)} %copy.81, f32[4,512]{1,0:T(4,128)S(1)} %fusion.52, f32[4,512]{1,0:T(4,128)S(1)} %get-tuple-element.95, f32[4,512,1280]{2,1,0:T(8,128)} %get-tuple-element.96, ...), kind=kOutput, calls=%fused_computation | convolution fusion | flops 1390801920 | bytes 19542036 | tf_op jit(solution)/shard_map/mqf,mpf->mqp/dot_general | solution.py:43
  219.0 2.8 copy.83
  221.8 4.3 all-to-all-start.2
  226.7 6.0 %fusion.10 = f32[4,1280,261]{1,2,0:T(8,128)S(1)} fusion(bf16[4,512,261]{2,1,0:T(8,128)(2,1)} %all-gather.5.cloned.1.call-done, f32[4,512]{1,0:T(4,128)S(1)} %fusion.52, f32[4,512,1280]{2,1,0:T(8,128)} %get-tuple-element.96, f32[4,512]{1,0:T(4,128)S(1)} %copy-done.23, pred[4,1280]{1,0:T(4,128)(4,1)S(1)} %copy-done.29), kind=kOutput, calls=%fused_computation.17 | convolution fusion | flops 1378877440 | bytes 16921600 | tf_op jit(solution)/shard_map/mqp,mqf->mpf/dot_general | solution.py:43
  232.7 7.6 %fusion.9 = (f32[4,1280]{1,0:T(4,128)S(1)}, f32[4,1280,261]{1,2,0:T(8,128)}) fusion(f32[261]{0:T(512)S(1)} %copy-done.31, f32[4,1280]{1,0:T(4,128)S(1)} %broadcast_multiply_fusion, bf16[4,1280,261]{1,0,2:T(4,128)(2,1)S(1)} %copy-done.3, f32[4,1280,261]{1,2,0:T(8,128)S(1)} %fusion.10, bf16[4,512,1280]{2,1,0:T(8,128)(2,1)} %copy-done.8, ...), kind=kOutput, calls=%fused_computation.16 | convolution fusion | flops 1376404480 | bytes 19717140 | tf_op jit(solution)/shard_map/mqp,mqf->mpf/dot_general | solution.py:43
  240.3 22.3 %all-to-all-done.2 = bf16[8,4,64,261]{3,2,1,0:T(8,128)(2,1)} async-done(((bf16[8,4,64,261]{3,2,1,0:T(8,128)(2,1)}), bf16[8,4,64,261]{3,2,1,0:T(8,128)(2,1)}, u32[]{:S(2)}, u32[]{:S(2)}) %all-to-all-start.2) | async-done | bytes 1069088 | tf_op jit(solution)/shard_map/all_to_all | solution.py:49
  266.5 4.5 fusion.7
  271.1 4.1 broadcast_add_fusion
  275.2 4.5 copy.84
  279.7 3.8 multiply_reduce_fusion.3
  285.3 59.2 %all-reduce.6 = (bf16[261,1024]{1,0:T(8,128)(2,1)}, f32[1024]{0:T(1024)}, f32[261]{0:T(512)}, f32[1024]{0:T(1024)}) all-reduce(f32[261,1024]{1,0:T(8,128)S(1)} %fusion.38, f32[1024]{0:T(1024)S(1)} %get-tuple-element.76, f32[261]{0:T(512)S(1)} %get-tuple-element.72, ...), channel_id=1, replica_groups=mesh['img'=4,'blk'=8] {'img','blk'}, use_global_device_ids=true, to_apply=%region_20.21 | all-reduce | flops 269573 | bytes 1622056 | tf_op jit(solution)/shard_map/psum | solution.py:118
  344.5 4.5 convolution_bitcast_fusion
  349.0 5.5 %copy.85 = f32[1024,1024]{1,0:T(8,128)} copy(f32[1024,1024]{0,1:T(8,128)} %convolution_bitcast_fusion) | data formatting | bytes 8388608
  355.8 3.5 fusion.80
  359.4 104.3 %all-reduce.5.cloned.1.call-done = (f32[1024,261]{0,1:T(8,128)}, f32[1024,1024]{1,0:T(8,128)}, f32[1024,1024]{1,0:T(8,128)}) async-done(((f32[1024,261]{0,1:T(8,128)}, f32[1024,1024]{1,0:T(8,128)}, f32[1024,1024]{1,0:T(8,128)}), (f32[1024,261]{0,1:T(8,128)}, f32[1024,1024]{1,0:T(8,128)}, f32[1024,1024]{1,0:T(8,128)})) %all-reduce.5.cloned.1.call-update) | async-done | bytes 9457680 | tf_op jit(solution)/shard_map/psum | solution.py:118
  463.7 4.8 %fusion.43 = f32[1024,1024]{1,0:T(8,128)} fusion(bf16[261,1024]{1,0:T(8,128)(2,1)} %param.18, f32[1024,261]{0,1:T(8,128)} %get-tuple-element.82), kind=kOutput, calls=%fused_computation.88 | convolution fusion | flops 547891200 | bytes 5797888 | tf_op jit(solution)/shard_map/dot_general | solution.py:27
  468.5 3.3 fusion.42
  (158 shorter events, 52.9 us)
Async XLA Ops:
  7.2 140.1 %copy-start = (bf16[1024,1024]{1,0:T(8,128)(2,1)S(1)}, bf16[1024,1024]{1,0:T(8,128)(2,1)}, u32[]{:S(2)}) copy-start(bf16[1024,1024]{1,0:T(8,128)(2,1)} %param.22) | copy-start | bytes 6291460
  7.2 56.6 %all-gather.3.cloned.1.call-start = ((), (), s32[]{:S(2)}) async-start(), calls=%async_computation.3 | async-start | bytes 1769472 | tf_op jit(solution)/shard_map/all_gather | solution.py:66
  13.2 8.1 %copy-start.42 = (s32[4]{0:T(128)S(1)}, s32[4]{0:T(128)}, u32[]{:S(2)}) copy-start(s32[4]{0:T(128)} %param.14) | copy-start | bytes 52
  13.2 50.6 %copy-start.30 = (f32[261]{0:T(512)S(1)}, f32[261]{0:T(512)}, u32[]{:S(2)}) copy-start(f32[261]{0:T(512)} %param.24) | copy-start | bytes 3136
  21.3 51.8 %copy-start.20 = (f32[4,1280]{1,0:T(4,128)}, f32[4,1280]{1,0:T(4,128)S(1)}, u32[]{:S(2)}) copy-start(f32[4,1280]{1,0:T(4,128)S(1)} %fusion.8) | copy-start | bytes 61444
  21.4 62.0 %copy-start.28 = (pred[4,1280]{1,0:T(4,128)(4,1)}, pred[4,1280]{1,0:T(4,128)(4,1)S(1)}, u32[]{:S(2)}) copy-start(pred[4,1280]{1,0:T(4,128)(4,1)S(1)} %broadcast_compare_fusion) | copy-start | bytes 15364
  73.1 131.7 %copy-start.22 = (f32[4,512]{1,0:T(4,128)}, f32[4,512]{1,0:T(4,128)S(1)}, u32[]{:S(2)}) copy-start(f32[4,512]{1,0:T(4,128)S(1)} %get-tuple-element.95) | copy-start | bytes 24580
  79.9 17.2 %all-to-all-start.1 = ((f32[8,1,512]{2,1,0:T(1,128)}), f32[8,1,512]{2,1,0:T(1,128)S(1)}, u32[]{:S(2)}, u32[]{:S(2)}) async-start(f32[8,1,512]{2,1,0:T(1,128)} %reshape.234), calls=%async_computation.1 | async-start | bytes 32768 | tf_op jit(solution)/shard_map/all_to_all | solution.py:49
  91.7 11.5 %copy-start.12 = (f32[4,64,1024]{2,1,0:T(8,128)S(1)}, f32[4,64,1024]{2,1,0:T(8,128)}, u32[]{:S(2)}) copy-start(f32[4,64,1024]{2,1,0:T(8,128)} %param.16) | copy-start | bytes 3145732
  97.1 42.6 %all-to-all-start = ((bf16[8,4,64,261]{3,2,1,0:T(8,128)(2,1)}), bf16[8,4,64,261]{3,2,1,0:T(8,128)(2,1)}, u32[]{:S(2)}, u32[]{:S(2)}) async-start(bf16[8,4,64,261]{3,2,1,0:T(8,128)(2,1)} %copy.74), calls=%async_computation | async-start | bytes 3145728 | tf_op jit(solution)/shard_map/all_to_all | solution.py:49
  103.1 101.7 %all-gather.5.cloned.1.call-start = ((), (), s32[]{:S(2)}) async-start(), calls=%async_computation.4 | async-start | bytes 1769472 | tf_op jit(solution)/shard_map/all_gather | solution.py:104
  105.6 48.9 %copy-start.40 = (f32[256]{0:T(256)}, f32[256]{0:T(256)S(1)}, u32[]{:S(2)}) copy-start(f32[256]{0:T(256)S(1)} %div.72) | copy-start | bytes 3076
  105.6 39.3 %copy-start.24 = (f32[1024]{0:T(1024)S(1)}, f32[1024]{0:T(1024)}, u32[]{:S(2)}) copy-start(f32[1024]{0:T(1024)} %param.25) | copy-start | bytes 12292
  204.8 11.0 %copy-start.31 = (f32[261]{0:T(512)S(1)}, f32[261]{0:T(512)}, u32[]{:S(2)}) copy-start(f32[261]{0:T(512)} %param.24) | copy-start | bytes 3136
  204.8 11.0 %copy-start.2 = (bf16[4,1280,261]{1,0,2:T(4,128)(2,1)S(1)}, bf16[4,1280,261]{1,0,2:T(4,128)(2,1)}, u32[]{:S(2)}) copy-start(bf16[4,1280,261]{1,0,2:T(4,128)(2,1)} %param.13) | copy-start | bytes 8017924
  217.5 8.9 %copy-start.6 = (f32[256,1024]{1,0:T(8,128)S(1)}, f32[256,1024]{1,0:T(8,128)}, u32[]{:S(2)}) copy-start(f32[256,1024]{1,0:T(8,128)} %bitcast_add_fusion) | copy-start | bytes 3145732
  217.5 8.9 %copy-start.41 = (f32[256]{0:T(256)S(1)}, f32[256]{0:T(256)}, u32[]{:S(2)}) copy-start(f32[256]{0:T(256)} %copy-done.40) | copy-start | bytes 3076
  219.0 7.7 %copy-start.23 = (f32[4,512]{1,0:T(4,128)S(1)}, f32[4,512]{1,0:T(4,128)}, u32[]{:S(2)}) copy-start(f32[4,512]{1,0:T(4,128)} %copy-done.22) | copy-start | bytes 24580
  221.8 40.8 %all-to-all-start.2 = ((bf16[8,4,64,261]{3,2,1,0:T(8,128)(2,1)}), bf16[8,4,64,261]{3,2,1,0:T(8,128)(2,1)}, u32[]{:S(2)}, u32[]{:S(2)}) async-start(bf16[8,4,64,261]{3,2,1,0:T(8,128)(2,1)} %copy.83), calls=%async_computation.2 | async-start | bytes 3145728 | tf_op jit(solution)/shard_map/all_to_all | solution.py:49
  226.1 237.6 %all-reduce.5.cloned.1.call-start = ((), (), s32[]{:S(2)}) async-start(), calls=%async_computation.5 | async-start | bytes 18939904 | tf_op jit(solution)/shard_map/psum | solution.py:118
  226.7 6.0 %copy-start.3 = (bf16[4,1280,261]{1,0,2:T(4,128)(2,1)S(1)}, bf16[4,1280,261]{1,0,2:T(4,128)(2,1)}, u32[]{:S(2)}) copy-start(bf16[4,1280,261]{1,0,2:T(4,128)(2,1)} %param.13) | copy-start | bytes 8017924
  232.7 31.6 %copy-start.5 = (bf16[4,64,1024]{2,1,0:T(8,128)(2,1)S(1)}, bf16[4,64,1024]{2,1,0:T(8,128)(2,1)}, u32[]{:S(2)}) copy-start(bf16[4,64,1024]{2,1,0:T(8,128)(2,1)} %param.15) | copy-start | bytes 1572868
  232.7 31.6 %copy-start.25 = (f32[1024]{0:T(1024)S(1)}, f32[1024]{0:T(1024)}, u32[]{:S(2)}) copy-start(f32[1024]{0:T(1024)} %param.23) | copy-start | bytes 12292
  232.7 31.6 %copy-start.27 = (f32[4,64]{1,0:T(4,128)S(1)}, f32[4,64]{1,0:T(4,128)}, u32[]{:S(2)}) copy-start(f32[4,64]{1,0:T(4,128)} %copy-done.26) | copy-start | bytes 3076
  232.7 31.6 %copy-start.38 = (f32[4,64]{1,0:T(4,128)S(1)}, f32[4,64]{1,0:T(4,128)}, u32[]{:S(2)}) copy-start(f32[4,64]{1,0:T(4,128)} %get-tuple-element.93) | copy-start | bytes 3076
  265.8 5.3 %copy-start.4 = (bf16[4,1280,261]{1,0,2:T(4,128)(2,1)S(1)}, bf16[4,1280,261]{1,0,2:T(4,128)(2,1)}, u32[]{:S(2)}) copy-start(bf16[4,1280,261]{1,0,2:T(4,128)(2,1)} %param.13) | copy-start | bytes 8017924
  275.2 4.5 copy-start.33
  279.7 5.6 %copy-start.39 = (f32[1024]{0:T(1024)S(1)}, f32[1024]{0:T(1024)}, u32[]{:S(2)}) copy-start(f32[1024]{0:T(1024)} %get-tuple-element.74) | copy-start | bytes 12292
  349.0 5.5 %copy-start.9 = (f32[256,1024]{1,0:T(8,128)S(1)}, f32[256,1024]{1,0:T(8,128)}, u32[]{:S(2)}) copy-start(f32[256,1024]{1,0:T(8,128)} %get-tuple-element.102) | copy-start | bytes 3145732
  463.7 4.9 %copy-start.7 = (f32[1024,261]{0,1:T(8,128)S(1)}, f32[1024,261]{0,1:T(8,128)}, u32[]{:S(2)}) copy-start(f32[1024,261]{0,1:T(8,128)} %get-tuple-element.82) | copy-start | bytes 3207172
  463.7 8.2 %copy-start.11 = (f32[1024,1024]{1,0:T(8,128)S(1)}, f32[1024,1024]{1,0:T(8,128)}, u32[]{:S(2)}) copy-start(f32[1024,1024]{1,0:T(8,128)} %get-tuple-element.112) | copy-start | bytes 12582916
  471.9 5.7 %copy-start.1 = (bf16[1024,1024]{1,0:T(8,128)(2,1)S(1)}, bf16[1024,1024]{1,0:T(8,128)(2,1)}, u32[]{:S(2)}) copy-start(bf16[1024,1024]{1,0:T(8,128)(2,1)} %param.22) | copy-start | bytes 6291460
  (17 other events, 42.8 us)
Sparse Core Ops, SparseCore 0:
  16.9 46.8 all-gather.2
  160.0 44.4 all-gather.4
  265.9 197.7 all-reduce.4
